TPU v7x, 128 devices: a whole 4x4x4 slice. The times are simulated.
128 devices in a mesh: orb: 16 (over z, y_lo, core), aux: 8 (over y_hi, x).
Axes of the slice: x: 4, y: 4 (y_hi: 2, y_lo: 2; y = y_hi * 2 + y_lo), z: 4, core: 2. Of those that a mesh axis runs over, the one named last changes fastest.
Arguments:
- three_center: bfloat16 [512, 128, 128, 128], P(('orb', 'aux')), may hold values from -0.5 to 0.5
- screening: int32 [512, 3], P(('orb', 'aux')), may hold values from -1 to 511, as said below
- density_factor: bfloat16 [65536, 128], P('orb'), may hold values from -0.23925781 to 0.23925781
- metric_inverse: bfloat16 [1024, 1024], replicated, may hold values from -1 to 1, as said below
Outputs:
- exchange_block: bfloat16 [2048, 256], P('orb')
Inputs may be any that keep to these rules, and one draw needn't show every extreme that they name: `screening`: A device's slots are 4 consecutive rows, devices in order of orb index then aux index. Column 0 equals the orb index and column 2 the aux index of the device holding the row. Column 1 is an orbital block, or -1 for an empty slot; empty slots follow the live ones, the live orbital blocks of a device are distinct, every device has 1 to 4 live slots, and some device has 4. `metric_inverse`: Symmetric.
All inputs are finite; a program needn't handle non-finite values.
Results may differ from a plain program's by a relative error of at most 0.0063.
Values may be sent and summed in bfloat16 or wider, within the bound.
A program may use at most 128 MiB of HBM per device.

v0:
```python
import jax
import jax.numpy as jnp
from jax import lax
from jax.sharding import PartitionSpec as P


def in_order(tiles, dim):
    lengths = list(tiles.shape[1:])
    lengths[dim] *= tiles.shape[0]
    return jnp.moveaxis(tiles, 0, dim).reshape(lengths)


def sent_to_all(x, axis):
    copies = jnp.broadcast_to(x, (lax.axis_size(axis), *x.shape))
    return lax.all_to_all(copies, axis, split_axis=0, concat_axis=0, tiled=True)


def gather_directly(x, axis, dim):
    return in_order(sent_to_all(x, axis), dim)


def from_behind(x, axis, by):
    length = lax.axis_size(axis)
    return lax.ppermute(x, axis, [(i, (i + by) % length) for i in range(length)])


def of_everyone(x, axis):
    everything = sent_to_all(x, axis)
    return jnp.sum(everything, axis=0)


def keep_same(current):
    return current


def contract_arrived(three_center, orbitals, arrived, running):
    slot_count = three_center.shape[0]

    def one_slot(slot_index, carried):
        inside = orbitals[slot_index] >= 0

        def add_tile(current):
            row_block = lax.dynamic_index_in_dim(arrived, slot_index, 0, keepdims=False)
            tile_now = lax.dynamic_index_in_dim(three_center, slot_index, 0, keepdims=False)
            return current + jnp.einsum(
                "mlp,li->mip", tile_now, row_block, preferred_element_type=jnp.float32
            )

        return lax.cond(inside, add_tile, keep_same, carried)

    return lax.fori_loop(0, slot_count, one_slot, running)


def on_device(three_center, screening, density_factor, metric_inverse):
    block_width = three_center.shape[1]
    slot_count = three_center.shape[0]
    occupied = density_factor.shape[1]
    orbitals = screening[:, 1]
    zero_start = jnp.zeros((block_width, occupied, block_width), jnp.float32)
    wanted_all = gather_directly(orbitals, "orb", 0)
    owned_count = density_factor.shape[0] // block_width
    local_index = wanted_all - lax.axis_index("orb") * owned_count
    owned_here = (wanted_all >= 0) & (local_index >= 0) & (local_index < owned_count)
    blocks_here = density_factor.reshape(owned_count, block_width, occupied)
    picked = blocks_here[jnp.clip(local_index, 0, owned_count - 1)]
    picked = jnp.where(owned_here[:, None, None], picked, jnp.zeros_like(picked))
    orb_count = lax.axis_size("orb")
    picked = picked.reshape(orb_count, slot_count * block_width, occupied)
    arrived = lax.all_to_all(picked, "orb", split_axis=0, concat_axis=0, tiled=True)
    arrived = arrived.reshape(orb_count, slot_count, block_width, occupied)
    owner_index = jnp.clip(orbitals // owned_count, 0, orb_count - 1)
    slot_ids = jnp.arange(slot_count, dtype=jnp.int32)
    arrived = arrived[owner_index, slot_ids]
    partial_half = contract_arrived(three_center, orbitals, arrived, zero_start)
    half_local = partial_half.astype(jnp.bfloat16)
    relaid = lax.all_to_all(half_local, "aux", split_axis=1, concat_axis=2, tiled=True)
    fitted_part = jnp.einsum(
        "miP,PQ->miQ", relaid, metric_inverse, preferred_element_type=jnp.float32
    )
    fitted = fitted_part.astype(jnp.bfloat16)
    following = from_behind(relaid, "orb", -1)
    diagonal = jnp.einsum("miq,niq->mn", fitted, relaid, preferred_element_type=jnp.float32)
    coupling = jnp.einsum("miq,niq->mn", fitted, following, preferred_element_type=jnp.float32)
    summed = of_everyone(jnp.concatenate([diagonal, coupling], axis=1), "aux")
    return summed.astype(jnp.bfloat16)


def solution(mesh):
    placed = (P(("orb", "aux"), None, None, None), P(("orb", "aux"), None), P("orb", None), P())
    return jax.shard_map(
        on_device, mesh=mesh, in_specs=placed, out_specs=P("orb", None), check_vma=False
    )
```

profile of v0, /device:TPU:1, one launch (start us, length us, event | category | flops | bytes accessed | tf_op | source)
XLA Modules:
  0.0 251.4 jit_solution(9100968181579657889)
XLA Ops:
  0.0 0.0 copy-start
  0.0 1.1 or_reduce_fusion
  1.1 0.6 broadcast_in_dim.29
  1.7 7.8 %all-to-all-start = ((s32[16,1,4]{2,1,0:T(1,128)}), s32[16,1,4]{2,1,0:T(1,128)S(1)}, u32[]{:S(2)}, u32[]{:S(2)}) async-start(s32[16,1,4]{2,1,0:T(1,128)} %broadcast_in_dim.29), calls=%async_computation | async-start | bytes 16384 | tf_op jit(solution)/shard_map/all_to_all | solution.py:15
  9.5 5.4 %all-to-all-done = s32[16,1,4]{2,1,0:T(1,128)S(1)} async-done(((s32[16,1,4]{2,1,0:T(1,128)}), s32[16,1,4]{2,1,0:T(1,128)S(1)}, u32[]{:S(2)}, u32[]{:S(2)}) %all-to-all-start) | async-done | bytes 288 | tf_op jit(solution)/shard_map/all_to_all | solution.py:15
  14.9 0.1 copy.26
  15.0 0.1 copy.29
  15.1 0.1 min.20
  15.2 0.1 copy.28
  15.3 0.1 broadcast_in_dim.30
  15.4 3.3 %gather_fusion = bf16[64,128,128]{2,1,0:T(8,128)(2,1)} fusion(bf16[32,128,128]{2,1,0:T(8,128)(2,1)} %bitcast.52, s32[1024]{0:T(1024)S(1)} %pad_clamp_fusion), kind=kCustom, calls=%fused_computation | custom fusion | bytes 4194560 | tf_op jit(solution)/shard_map/gather | solution.py:65
  18.8 4.4 %bitcast_select_fusion = bf16[16,512,128]{2,1,0:T(8,128)(2,1)} fusion(pred[16,512]{1,0:T(8,128)(4,1)S(1)} %bitcast.53, bf16[16,512,128]{2,1,0:T(8,128)(2,1)} %bitcast.51), kind=kLoop, calls=%fused_computation.13 | loop fusion | flops 1048576 | bytes 4202496 | tf_op jit(solution)/shard_map/jit(_where)/select_n | solution.py:66
  23.2 4.8 %all-to-all-start.1 = ((bf16[16,512,128]{2,1,0:T(8,128)(2,1)}), bf16[16,512,128]{2,1,0:T(8,128)(2,1)}, u32[]{:S(2)}, u32[]{:S(2)}) async-start(bf16[16,512,128]{2,1,0:T(8,128)(2,1)} %bitcast_select_fusion), calls=%async_computation.1 | async-start | bytes 4194304 | tf_op jit(solution)/shard_map/all_to_all | solution.py:69
  28.1 27.3 %all-to-all-done.1 = bf16[16,512,128]{2,1,0:T(8,128)(2,1)} async-done(((bf16[16,512,128]{2,1,0:T(8,128)(2,1)}), bf16[16,512,128]{2,1,0:T(8,128)(2,1)}, u32[]{:S(2)}, u32[]{:S(2)}) %all-to-all-start.1) | async-done | bytes 2097184 | tf_op jit(solution)/shard_map/all_to_all | solution.py:69
  55.4 2.2 gather_fusion.1
  57.5 0.1 copy.30
  57.7 4.3 %broadcast_in_dim.28 = f32[128,128,128]{2,1,0:T(8,128)} broadcast(f32[]{:T(128)} %constant.61.clone.1), dimensions={} | broadcast | bytes 8388612 | tf_op jit(solution)/shard_map/broadcast_in_dim | solution.py:59
  62.0 41.5 %while.16 = (s32[]{:T(128)}, f32[128,128,128]{2,1,0:T(8,128)}, s32[4]{0:T(128)S(1)}, bf16[4,128,128]{1,2,0:T(8,128)(2,1)S(1)}, bf16[4,128,128,128]{3,2,1,0:T(8,128)(2,1)}, /*index=5*/s32[]{:T(128)}, s32[1]{0:T(128)}) while((s32[]{:T(128)}, f32[128,128,128]{2,1,0:T(8,128)}, s32[4]{0:T(128)S(1)}, bf16[4,128,128]{1,2,0:T(8,128)(2,1)S(1)}, ...), condition=%wide.region_3.4_spmd, body=%wide.region_0.3_spmd.sunk | while | flops 538968064 | bytes 21005488 | solution.py:51
  62.0 0.6 dynamic_slice.26
  63.2 9.2 %conditional.2 = (f32[128,128,128]{2,1,0:T(8,128)}) conditional(s32[]{:T(128)} %bitcast.48, f32[128,128,128]{2,1,0:T(8,128)} %get-tuple-element.191, (s32[]{:T(128)}, bf16[4,128,128]{1,2,0:T(8,128)(2,1)S(1)}, bf16[4,128,128,128]{3,2,1,0:T(8,128)(2,1)}, f32[128,128,128]{2,1,0:T(8,128)}) %tuple.44), branch_computations={%region_1.1_spmd, %region_2.2_spmd} | conditional | flops 538968064 | bytes 21005354 | solution.py:49
  63.2 9.1 %bitcast_add_fusion = f32[128,128,128]{2,1,0:T(8,128)} fusion(f32[128,128,128]{2,1,0:T(8,128)} %get-tuple-element.108, bf16[4,128,128,128]{3,2,1,0:T(8,128)(2,1)} %get-tuple-element.111, s32[]{:T(128)S(6)} %select_n.32, bf16[4,128,128]{1,2,0:T(8,128)(2,1)S(1)} %get-tuple-element.109), kind=kOutput, calls=%fused_computation.2 | convolution fusion | flops 538968064 | bytes 21005312 | tf_op jit(solution)/shard_map/while/body/eval_jaxpr/cond/branch_1_fun/mlp,li->mip/dot_general | solution.py:45
  72.3 0.6 dynamic_slice.26
  73.6 9.2 %conditional.2 = (f32[128,128,128]{2,1,0:T(8,128)}) conditional(s32[]{:T(128)} %bitcast.48, f32[128,128,128]{2,1,0:T(8,128)} %get-tuple-element.191, (s32[]{:T(128)}, bf16[4,128,128]{1,2,0:T(8,128)(2,1)S(1)}, bf16[4,128,128,128]{3,2,1,0:T(8,128)(2,1)}, f32[128,128,128]{2,1,0:T(8,128)}) %tuple.44), branch_computations={%region_1.1_spmd, %region_2.2_spmd} | conditional | flops 538968064 | bytes 21005354 | solution.py:49
  73.6 9.1 %bitcast_add_fusion = f32[128,128,128]{2,1,0:T(8,128)} fusion(f32[128,128,128]{2,1,0:T(8,128)} %get-tuple-element.108, bf16[4,128,128,128]{3,2,1,0:T(8,128)(2,1)} %get-tuple-element.111, s32[]{:T(128)S(6)} %select_n.32, bf16[4,128,128]{1,2,0:T(8,128)(2,1)S(1)} %get-tuple-element.109), kind=kOutput, calls=%fused_computation.2 | convolution fusion | flops 538968064 | bytes 21005312 | tf_op jit(solution)/shard_map/while/body/eval_jaxpr/cond/branch_1_fun/mlp,li->mip/dot_general | solution.py:45
  82.7 0.6 dynamic_slice.26
  83.9 9.2 %conditional.2 = (f32[128,128,128]{2,1,0:T(8,128)}) conditional(s32[]{:T(128)} %bitcast.48, f32[128,128,128]{2,1,0:T(8,128)} %get-tuple-element.191, (s32[]{:T(128)}, bf16[4,128,128]{1,2,0:T(8,128)(2,1)S(1)}, bf16[4,128,128,128]{3,2,1,0:T(8,128)(2,1)}, f32[128,128,128]{2,1,0:T(8,128)}) %tuple.44), branch_computations={%region_1.1_spmd, %region_2.2_spmd} | conditional | flops 538968064 | bytes 21005354 | solution.py:49
  84.0 9.1 %bitcast_add_fusion = f32[128,128,128]{2,1,0:T(8,128)} fusion(f32[128,128,128]{2,1,0:T(8,128)} %get-tuple-element.108, bf16[4,128,128,128]{3,2,1,0:T(8,128)(2,1)} %get-tuple-element.111, s32[]{:T(128)S(6)} %select_n.32, bf16[4,128,128]{1,2,0:T(8,128)(2,1)S(1)} %get-tuple-element.109), kind=kOutput, calls=%fused_computation.2 | convolution fusion | flops 538968064 | bytes 21005312 | tf_op jit(solution)/shard_map/while/body/eval_jaxpr/cond/branch_1_fun/mlp,li->mip/dot_general | solution.py:45
  93.1 0.6 dynamic_slice.26
  94.3 9.2 %conditional.2 = (f32[128,128,128]{2,1,0:T(8,128)}) conditional(s32[]{:T(128)} %bitcast.48, f32[128,128,128]{2,1,0:T(8,128)} %get-tuple-element.191, (s32[]{:T(128)}, bf16[4,128,128]{1,2,0:T(8,128)(2,1)S(1)}, bf16[4,128,128,128]{3,2,1,0:T(8,128)(2,1)}, f32[128,128,128]{2,1,0:T(8,128)}) %tuple.44), branch_computations={%region_1.1_spmd, %region_2.2_spmd} | conditional | flops 538968064 | bytes 21005354 | solution.py:49
  94.3 9.1 %bitcast_add_fusion = f32[128,128,128]{2,1,0:T(8,128)} fusion(f32[128,128,128]{2,1,0:T(8,128)} %get-tuple-element.108, bf16[4,128,128,128]{3,2,1,0:T(8,128)(2,1)} %get-tuple-element.111, s32[]{:T(128)S(6)} %select_n.32, bf16[4,128,128]{1,2,0:T(8,128)(2,1)S(1)} %get-tuple-element.109), kind=kOutput, calls=%fused_computation.2 | convolution fusion | flops 538968064 | bytes 21005312 | tf_op jit(solution)/shard_map/while/body/eval_jaxpr/cond/branch_1_fun/mlp,li->mip/dot_general | solution.py:45
  103.5 8.2 %copy.38 = bf16[128,128,128]{2,0,1:T(8,128)(2,1)S(1)} copy(f32[128,128,128]{2,1,0:T(8,128)} %get-tuple-element.119) | data formatting | bytes 12582912 | tf_op jit(solution)/shard_map/while | solution.py:51
  111.7 55.5 %all_to_all.34 = bf16[128,128,128]{2,0,1:T(8,128)(2,1)S(1)} all-to-all(bf16[128,128,128]{2,0,1:T(8,128)(2,1)S(1)} %copy.38), channel_id=1, replica_groups=mesh['orb'=16,'aux'=8] {'aux'}, dimensions={1} | all-to-all | bytes 8388608 | tf_op jit(solution)/shard_map/all_to_all | solution.py:76
  167.2 5.5 %copy.39 = bf16[128,8,16,128]{3,1,0,2:T(8,128)(2,1)} copy(bf16[128,8,16,128]{3,0,2,1:T(8,128)(2,1)S(1)} %bitcast.49) | data formatting | bytes 8388608 | tf_op jit(solution)/shard_map/all_to_all | solution.py:76
  172.7 7.3 %all_to_all.28 = bf16[128,16,1024]{2,0,1:T(8,128)(2,1)} reshape(bf16[128,16,8,128]{3,2,0,1:T(8,128)(2,1)} %bitcast.50) | data formatting | bytes 8388608 | tf_op jit(solution)/shard_map/all_to_all | solution.py:76
  180.1 0.0 copy-start.1
  180.1 2.3 collective-permute-start
  182.4 0.0 copy-done
  182.4 6.9 %convolution_convert_fusion = bf16[128,16,1024]{2,0,1:T(8,128)(2,1)S(1)} fusion(bf16[128,16,1024]{2,0,1:T(8,128)(2,1)} %all_to_all.28, bf16[1024,1024]{1,0:T(8,128)(2,1)S(1)} %copy-done), kind=kOutput, calls=%fused_computation.11 | convolution fusion | flops 4297064448 | bytes 10485760 | tf_op jit(solution)/shard_map/miP,PQ->miQ/dot_general | solution.py:77
  189.3 0.0 copy-done.1
  189.3 1.2 convolution_bitcast_fusion.1
  190.5 43.3 %collective-permute-done = bf16[128,16,1024]{2,0,1:T(8,128)(2,1)S(1)} collective-permute-done((bf16[128,16,1024]{2,0,1:T(8,128)(2,1)}, bf16[128,16,1024]{2,0,1:T(8,128)(2,1)S(1)}, u32[]{:S(2)}, u32[]{:S(2)}) %collective-permute-start) | collective-permute-done | bytes 4194336 | tf_op jit(solution)/shard_map/ppermute | solution.py:24
  233.8 1.2 convolution_bitcast_fusion
  235.1 0.1 copy.33
  235.2 0.1 broadcast_in_dim.34
  235.3 15.4 %all_to_all.35 = f32[8,128,256]{2,1,0:T(8,128)S(1)} all-to-all(f32[8,128,256]{2,1,0:T(8,128)S(1)} %broadcast_in_dim.34), channel_id=1, replica_groups=mesh['orb'=16,'aux'=8] {'aux'}, dimensions={0} | all-to-all | bytes 2097152 | tf_op jit(solution)/shard_map/all_to_all | solution.py:15
  250.7 0.7 reduce_sum.9
  (6 shorter events, 0.0 us)
Async XLA Ops:
  0.0 182.4 %copy-start = (bf16[1024,1024]{1,0:T(8,128)(2,1)S(1)}, bf16[1024,1024]{1,0:T(8,128)(2,1)}, u32[]{:S(2)}) copy-start(bf16[1024,1024]{1,0:T(8,128)(2,1)} %param.11) | copy-start | bytes 6291460
  1.7 13.3 %all-to-all-start = ((s32[16,1,4]{2,1,0:T(1,128)}), s32[16,1,4]{2,1,0:T(1,128)S(1)}, u32[]{:S(2)}, u32[]{:S(2)}) async-start(s32[16,1,4]{2,1,0:T(1,128)} %broadcast_in_dim.29), calls=%async_computation | async-start | bytes 16384 | tf_op jit(solution)/shard_map/all_to_all | solution.py:15
  23.2 32.2 %all-to-all-start.1 = ((bf16[16,512,128]{2,1,0:T(8,128)(2,1)}), bf16[16,512,128]{2,1,0:T(8,128)(2,1)}, u32[]{:S(2)}, u32[]{:S(2)}) async-start(bf16[16,512,128]{2,1,0:T(8,128)(2,1)} %bitcast_select_fusion), calls=%async_computation.1 | async-start | bytes 4194304 | tf_op jit(solution)/shard_map/all_to_all | solution.py:69
  180.1 9.2 %copy-start.1 = (bf16[128,16,1024]{2,0,1:T(8,128)(2,1)S(1)}, bf16[128,16,1024]{2,0,1:T(8,128)(2,1)}, u32[]{:S(2)}) copy-start(bf16[128,16,1024]{2,0,1:T(8,128)(2,1)} %all_to_all.28) | copy-start | bytes 12582916
  180.1 53.8 %collective-permute-start = (bf16[128,16,1024]{2,0,1:T(8,128)(2,1)}, bf16[128,16,1024]{2,0,1:T(8,128)(2,1)S(1)}, u32[]{:S(2)}, u32[]{:S(2)}) collective-permute-start(bf16[128,16,1024]{2,0,1:T(8,128)(2,1)} %all_to_all.28), channel_id=1, source_target_pairs={{0,120},{8,0},{16,8},{24,16},{32,24},{40,32},{48,40},{56,48},{64,5... | collective-permute-start | bytes 12582920 | tf_op jit(solution)/shard_map/ppermute | solution.py:24
where the time goes:
time: 252 us; the launch traced here: 251 us
  waiting for transfers between devices  76 us (30%)
  blocking collectives  70.9 us (28%)
  matrix products  45.9 us (18%)
  local copies, waits for them, and re-layouts  34.7 us (14%)
  starting transfers between devices  15 us (6%)
  other arithmetic  6.22 us (2%)
  loops' own time  2.6 us (1%)
    all_to_all x1, blocking collectives, on_device(): lax.all_to_all(half_local, 'aux', split_axis=1, concat_axis=2, tiled=True)  55.5 us
    ppermute x1, waiting for transfers between devices, from_behind(): lax.ppermute(x, axis, [(i, (i + by) % length) for i in range(length)])  43.3 us
    dot_general x4, matrix products, add_tile(): jnp.einsum('mlp,li->mip', tile_now, row_block, preferred_element_type=jnp...  36.5 us
    all_to_all x1, waiting for transfers between devices, on_device(): lax.all_to_all(picked, 'orb', split_axis=0, concat_axis=0, tiled=True)  27.3 us
    all_to_all x1, blocking collectives, sent_to_all(): return lax.all_to_all(copies, axis, split_axis=0, concat_axis=0, tiled=True)  15.4 us
    all_to_all x2, local copies, waits for them, and re-layouts, on_device(): lax.all_to_all(half_local, 'aux', split_axis=1, concat_axis=2, tiled=True)  12.9 us
    while x2, local copies, waits for them, and re-layouts, contract_arrived(): return lax.fori_loop(0, slot_count, one_slot, running)  8.37 us
    all_to_all x1, starting transfers between devices, sent_to_all(): return lax.all_to_all(copies, axis, split_axis=0, concat_axis=0, tiled=True)  7.84 us
  transfers between devices with their start and end apart: 3, of which 3 were waited for; matrix products, arithmetic and copies ran while one was open for 3% of the time, Pallas kernels for 0%

commit v1 on v0

v1 whole, which is shorter than its diff:
```python
import jax
import jax.numpy as jnp
from jax import lax
from jax.experimental import pallas as pl
from jax.experimental.pallas import tpu as pltpu
from jax.sharding import PartitionSpec as P

MESH = pl.DeviceIdType.MESH
B = 128
F32 = jnp.float32
BF16 = jnp.bfloat16


def place():
    orb, aux = lax.axis_index("orb"), lax.axis_index("aux")
    return aux % 4, (aux // 4) * 2 + (orb // 2) % 2, orb // 4, orb % 2


def device(x, y, z, c):
    x, y, z = (x + 4) % 4, (y + 4) % 4, (z + 4) % 4
    return (z * 4 + (y % 2) * 2 + c, (y // 2) * 4 + x)


def lanes(parts):
    return jnp.concatenate(parts, axis=1)


def rows(parts):
    return jnp.concatenate(parts, axis=0)


def kernel(
    t_hbm, scr_ref, d_hbm, j_hbm, o_ref,
    tiles, metric, owned, wants, wants_s, y_out, y_in, z_out, z_in, factor_t, perm,
    half, mid_x, mid_y, own, foll, total, red_in, gathered,
    t_sem, j_sem, d_sem, sib_sem, w_sem, ws_sem, y_sem, z_sem, s1_sem, s2_sem, l1_sem, l2_sem, f_sem, r_sem, g_sem,
):
    x, y, z, c = place()

    load_d = pltpu.make_async_copy(d_hbm, owned.at[pl.ds(c * 32, 32)], d_sem)
    load_d.start()
    load_t = []
    for g in range(8):
        span = pl.ds(g * 16, 16)
        load_t.append(pltpu.make_async_copy(t_hbm.at[:, span], tiles.at[:, span], t_sem.at[g]))
    load_j = pltpu.make_async_copy(j_hbm, metric, j_sem)
    for copy in load_t:
        copy.start()
    load_j.start()

    wants[0, z, pl.ds(0, 4), pl.ds(0, 3)] = scr_ref[...]

    plane = [(dx, dy) for dx in range(4) for dy in range(4) if (dx, dy) != (0, 0)]
    above = [(dy, dz) for dy in (0, 1, 3) for dz in (1, 2, 3)]
    barrier = pltpu.get_barrier_semaphore()
    peers = [device(x, y, z, 1 - c), device(x, y, z + 2 * c - 1, 1 - c)]
    peers += [device(x, y + dy, z + dz, c) for dy, dz in above]
    peers += [device(x + dx, y + dy, z, c) for dx, dy in plane]
    for peer in peers:
        pl.semaphore_signal(barrier, inc=1, device_id=peer, device_id_type=MESH)
    r = lax.broadcasted_iota(jnp.int32, (256, 256), 0)
    k = lax.broadcasted_iota(jnp.int32, (256, 256), 1)
    perm[...] = jnp.where((r % 16) * 16 + r // 16 == k, 1.0, 0.0).astype(BF16)
    pl.semaphore_wait(barrier, len(peers))

    def remote(src, dst, send, recv, peer):
        copy = pltpu.make_async_remote_copy(
            src_ref=src, dst_ref=dst, send_sem=send, recv_sem=recv, device_id=peer, device_id_type=MESH
        )
        copy.start()
        return copy

    sent = []

    want_copies = []
    for n, (dy, dz) in enumerate([(1, 0), (3, 0)] + above):
        slot = {0: 0, 1: 1, 3: 2}[dy]
        want_copies.append(
            remote(wants.at[0, z], wants.at[slot, z], w_sem.at[0, n], w_sem.at[1, n], device(x, y + dy, z + dz, c))
        )
    span = pl.ds(c * 32, 32)
    sibling = remote(d_hbm, owned.at[span], sib_sem.at[0], sib_sem.at[1], device(x, y, z, 1 - c))
    for copy in want_copies:
        copy.wait()
    to_scalar = pltpu.make_async_copy(wants, wants_s, ws_sem)
    to_scalar.start()
    load_d.wait()
    sibling.wait()
    to_scalar.wait()

    first = (z * 4 + (y % 2) * 2) * 32

    def pick(column, zz, slot):
        block = wants_s[column, zz, slot, 1] - first
        inside = (block >= 0) & (block < 64)
        found = owned[jnp.clip(block, 0, 63)]
        return jnp.where(inside, found, jnp.zeros_like(found))

    y_copies = []
    for sub in range(2):
        for way in range(2):
            @pl.loop(0, 4)
            def _(zz):
                y_out[sub, way, zz] = pick(2 - way, zz, way * 2 + sub)

            y_copies.append(
                remote(
                    y_out.at[sub, way], y_in.at[sub, way], y_sem.at[0, sub, way], y_sem.at[1, sub, way],
                    device(x, y + 1 - 2 * way, z, c),
                )
            )
    z_copies = []
    for sub in range(2):
        for way in range(2):
            y_copies[sub * 2 + way].wait()

            @pl.loop(0, 4)
            def _(zz):
                z_out[sub, zz, way] = pick(0, zz, way * 2 + sub) + y_in[sub, way, zz]

        for dz in (2, 1, 3):
            z_copies.append(
                remote(
                    z_out.at[sub, (z + dz) % 4], z_in.at[sub, dz - 1], z_sem.at[0, sub, dz], z_sem.at[1, sub, dz],
                    device(x, y, z + dz, c),
                )
            )
    for copy in z_copies:
        copy.wait()
    for slot in range(4):
        way, sub = slot // 2, slot % 2
        block = z_out[sub, z, way]
        for dz in range(3):
            block = block + z_in[sub, dz, way]
        factor_t[:, pl.ds(slot * B, B)] = block.astype(F32).T.astype(BF16)

    for copy in load_t:
        copy.wait()

    @pl.loop(0, 8)
    def _(g):
        made = []
        for pair in range(8):
            m = g * 16 + pair * 2
            right = rows([lanes([tiles[t, m], tiles[t, m + 1]]) for t in range(4)])
            out = jnp.dot(factor_t[...], right, preferred_element_type=F32).astype(BF16)
            made += [out[:, :B], out[:, B:]]
        for group in range(0, 8, 2):
            stack = lanes([rows([one[(group + e) * 16:(group + e + 1) * 16] for one in made]) for e in range(2)])
            turned = jnp.dot(perm[...], stack, preferred_element_type=F32).astype(BF16)
            for e in range(2):
                for i in range(16):
                    half[(group + e) * 16 + i, pl.ds(pl.multiple_of(g * 16, 16), 16), :] = turned[
                        i * 16:(i + 1) * 16, e * B:(e + 1) * B
                    ]

    def first_hop(chunk):
        n, odd = chunk // 2, chunk % 2
        at = y if odd else x
        land = mid_y.at[n, y // 2, y % 2] if odd else mid_x.at[n, x]
        copies = []
        for d in (2, 1, 3):
            there = (at + d) % 4
            peer = device(x, y + d, z, c) if odd else device(x + d, y, z, c)
            copies.append(
                remote(half.at[pl.ds(chunk * 16 + there * 4, 4)], land, s1_sem.at[0, chunk, d], s1_sem.at[1, chunk, d], peer)
            )
        stays = pltpu.make_async_copy(half.at[pl.ds(chunk * 16 + at * 4, 4)], land, l1_sem.at[chunk])
        stays.start()
        return copies + [stays]

    def second_hop(chunk):
        n, odd = chunk // 2, chunk % 2
        at = x if odd else y
        land = own.at[chunk, :, :, x] if odd else own.at[chunk, y // 2, y % 2]
        copies = []
        for d in (2, 1, 3):
            there = (at + d) % 4
            peer = device(x + d, y, z, c) if odd else device(x, y + d, z, c)
            source = mid_y.at[n, :, :, there] if odd else mid_x.at[n, :, there]
            copies.append(remote(source, land, s2_sem.at[0, chunk, d], s2_sem.at[1, chunk, d], peer))
        source = mid_y.at[n, :, :, at] if odd else mid_x.at[n, :, at]
        stays = pltpu.make_async_copy(source, land, l2_sem.at[chunk])
        stays.start()
        return copies + [stays]

    def follow(chunk):
        a = remote(
            own.at[chunk, :, 1 - c], foll.at[chunk, 0], f_sem.at[0, chunk, 0], f_sem.at[1, chunk, 0], device(x, y, z, 1 - c)
        )
        b = remote(
            own.at[chunk, :, c], foll.at[chunk, 1], f_sem.at[0, chunk, 1], f_sem.at[1, chunk, 1],
            device(x, y, z - (1 - c), 1 - c),
        )
        return [a, b]

    def done(copies):
        for copy in copies:
            copy.wait()

    def own_rows(chunk, s):
        return lanes([own[chunk, h, s, e] for h in range(2) for e in range(4)])

    def foll_rows(chunk, s):
        return lanes([foll[chunk, s, h, e] for h in range(2) for e in range(4)])

    total[...] = jnp.zeros_like(total)

    def finish(pair, hops):
        follows = []
        for e in range(2):
            done(hops[e])
            follows += follow(pair * 2 + e)
        fitted = []
        for e in range(2):
            stack = rows([own_rows(pair * 2 + e, s) for s in range(2)])
            fitted.append(jnp.dot(stack, metric[...], preferred_element_type=F32).astype(BF16))
        done(follows)
        for e in range(2):
            for s in range(2):
                right = rows([own_rows(pair * 2 + e, s), foll_rows(pair * 2 + e, s)])
                total[s] += lax.dot_general(
                    fitted[e][s * B:(s + 1) * B], right, (((1,), (1,)), ((), ())), preferred_element_type=F32
                )

    load_j.wait()
    hop1 = {n: first_hop(n) for n in range(4)}
    hop2 = {}
    for pair in range(4):
        for e in range(2):
            done(hop1[pair * 2 + e])
            hop2[pair * 2 + e] = second_hop(pair * 2 + e)
        if pair < 2:
            for e in range(2):
                hop1[pair * 2 + 4 + e] = first_hop(pair * 2 + 4 + e)
        if pair > 0:
            finish(pair - 1, [hop2[pair * 2 - 2], hop2[pair * 2 - 1]])
    finish(3, [hop2[6], hop2[7]])

    def share(xx, yy):
        return pl.ds(pl.multiple_of((((yy + 4) % 4) // 2 * 4 + (xx + 4) % 4) * 16, 16), 16)

    parts = []
    for n, (dx, dy) in enumerate(plane):
        parts.append(
            remote(
                total.at[(y + dy) % 2, share(x + dx, y + dy)], red_in.at[n], r_sem.at[0, n], r_sem.at[1, n],
                device(x + dx, y + dy, z, c),
            )
        )
    result = total[y % 2, share(x, y), :]
    done(parts)
    for n in range(len(plane)):
        result = result + red_in[n]
    gathered[share(x, y), :] = result.astype(BF16)
    parts = []
    for n, (dx, dy) in enumerate([p for p in plane if p[1] % 2 == 0]):
        parts.append(
            remote(
                gathered.at[share(x, y)], gathered.at[share(x, y)], g_sem.at[0, n], g_sem.at[1, n],
                device(x + dx, y + dy, z, c),
            )
        )
    done(parts)
    o_ref[...] = gathered[...]


def on_device(three_center, screening, density_factor, metric_inverse):
    dma = pltpu.SemaphoreType.DMA
    return pl.pallas_call(
        kernel,
        out_shape=jax.ShapeDtypeStruct((B, 2 * B), BF16),
        in_specs=[
            pl.BlockSpec(memory_space=pl.ANY),
            pl.BlockSpec(memory_space=pltpu.VMEM),
            pl.BlockSpec(memory_space=pl.ANY),
            pl.BlockSpec(memory_space=pl.ANY),
        ],
        out_specs=pl.BlockSpec(memory_space=pltpu.VMEM),
        scratch_shapes=[
            pltpu.VMEM((4, B, B, B), BF16),
            pltpu.VMEM((1024, 1024), BF16),
            pltpu.VMEM((64, B, B), BF16),
            pltpu.VMEM((3, 4, 8, B), jnp.int32),
            pltpu.SMEM((3, 4, 8, B), jnp.int32),
            pltpu.VMEM((2, 2, 4, B, B), BF16),
            pltpu.VMEM((2, 2, 4, B, B), BF16),
            pltpu.VMEM((2, 4, 2, B, B), BF16),
            pltpu.VMEM((2, 3, 2, B, B), BF16),
            pltpu.VMEM((B, 4 * B), BF16),
            pltpu.VMEM((256, 256), BF16),
            pltpu.VMEM((B, B, B), BF16),
            pltpu.VMEM((4, 4, 4, B, B), BF16),
            pltpu.VMEM((4, 2, 2, 4, B, B), BF16),
            pltpu.VMEM((8, 2, 2, 4, B, B), BF16),
            pltpu.VMEM((8, 2, 2, 4, B, B), BF16),
            pltpu.VMEM((2, B, 2 * B), F32),
            pltpu.VMEM((15, 16, 2 * B), F32),
            pltpu.VMEM((B, 2 * B), BF16),
            dma((8,)),
            dma,
            dma,
            dma((2,)),
            dma((2, 11)),
            dma,
            dma((2, 2, 2)),
            dma((2, 2, 4)),
            dma((2, 8, 4)),
            dma((2, 8, 4)),
            dma((8,)),
            dma((8,)),
            dma((2, 8, 2)),
            dma((2, 15)),
            dma((2, 7)),
        ],
        compiler_params=pltpu.CompilerParams(
            collective_id=0, has_side_effects=True, vmem_limit_bytes=56 * 1024 * 1024
        ),
        cost_estimate=pl.CostEstimate(flops=8_000_000_000, bytes_accessed=20_000_000, transcendentals=0),
    )(three_center, screening, density_factor.reshape(-1, B, B), metric_inverse)


def solution(mesh):
    placed = (P(("orb", "aux"), None, None, None), P(("orb", "aux"), None), P("orb", None), P())
    return jax.shard_map(
        on_device, mesh=mesh, in_specs=placed, out_specs=P("orb", None), check_vma=False
    )
```

time: 252 us -> 102 us (0.40)
  Pallas kernels: 0 us -> 101 us
  waiting for transfers between devices: 76 us -> 0 us
  blocking collectives: 70.9 us -> 0 us
  matrix products: 45.9 us -> 0 us
  local copies, waits for them, and re-layouts: 34.7 us -> 1.47 us
  starting transfers between devices: 15 us -> 0 us
  other arithmetic: 6.22 us -> 0 us
  loops' own time: 2.6 us -> 0 us
    pallas_call x0 -> x1, Pallas kernels: none -> 101 us  [on_device(): pl.pallas_call(kernel, out_shape=jax.ShapeDtypeStruct((B, 2 * B), BF16),...]
    all_to_all x2 -> x0, blocking collectives: 70.9 us -> none  [the longest x1 55.5 us: on_device(): lax.all_to_all(half_local, 'aux', split_axis=1, concat_axis=2, tiled=True)]
    dot_general x7 -> x0, matrix products: 45.9 us -> none  [the longest x4 36.5 us: add_tile(): jnp.einsum('mlp,li->mip', tile_now, row_block, preferred_element_type=jnp...]
    ppermute x1 -> x0, waiting for transfers between devices: 43.3 us -> none  [from_behind(): lax.ppermute(x, axis, [(i, (i + by) % length) for i in range(length)])]
    all_to_all x2 -> x0, waiting for transfers between devices: 32.7 us -> none  [the longest x1 27.3 us: on_device(): lax.all_to_all(picked, 'orb', split_axis=0, concat_axis=0, tiled=True)]
    all_to_all x3 -> x0, local copies, waits for them, and re-layouts: 13 us -> none  [the longest x2 12.9 us: on_device(): lax.all_to_all(half_local, 'aux', split_axis=1, concat_axis=2, tiled=True)]
    all_to_all x2 -> x0, starting transfers between devices: 12.7 us -> none  [the longest x1 7.84 us: sent_to_all(): return lax.all_to_all(copies, axis, split_axis=0, concat_axis=0, tiled=True)]
    while x2 -> x0, local copies, waits for them, and re-layouts: 8.37 us -> none  [contract_arrived(): return lax.fori_loop(0, slot_count, one_slot, running)]
  transfers between devices with their start and end apart: 3 -> 0, of which waited for: 3 -> 0; matrix products, arithmetic and copies ran while one was open for 3% -> 0% of each run, Pallas kernels for 0% -> 0%
where the time goes in v1:
time: 102 us
  Pallas kernels  101 us (99%)
  local copies, waits for them, and re-layouts  1.47 us (1%)
    pallas_call x1, Pallas kernels, on_device(): pl.pallas_call(kernel, out_shape=jax.ShapeDtypeStruct((B, 2 * B), BF16),...  101 us

profile of v1, /device:TPU:1, one launch (start us, length us, event | category | flops | bytes accessed | tf_op | source)
XLA Modules:
  0.0 102.0 jit_solution(13622236311455223151)
XLA Ops:
  0.0 100.5 %shard_map.46 = bf16[128,256]{1,0:T(8,128)(2,1)} custom-call(bf16[4,128,128,128]{3,2,1,0:T(8,128)(2,1)} %t_hbm.1, s32[4,3]{1,0:T(4,128)} %scr_ref.1, bf16[32,128,128]{2,1,0:T(8,128)(2,1)} %bitcast.1, bf16[1024,1024]{1,0:T(8,128)(2,1)} %j_hbm.1), custom_call_target="tpu_custom_call" | custom-call | flops 8000000000 | bytes 20000000 | tf_op jit(solution)/shard_map/pallas_call | solution.py:270
  100.5 1.5 %copy.6 = bf16[128,256]{1,0:T(8,128)(2,1)} copy(bf16[128,256]{1,0:T(8,128)(2,1)} %shard_map.46) | data formatting | bytes 131072

commit v2 on v1

v2 whole, which is shorter than its diff:
```python
import jax
import jax.numpy as jnp
from jax import lax
from jax.experimental import pallas as pl
from jax.experimental.pallas import tpu as pltpu
from jax.sharding import PartitionSpec as P

MESH = pl.DeviceIdType.MESH
B = 128
F32 = jnp.float32
BF16 = jnp.bfloat16


def place():
    orb, aux = lax.axis_index("orb"), lax.axis_index("aux")
    return aux % 4, (aux // 4) * 2 + (orb // 2) % 2, orb // 4, orb % 2


def device(x, y, z, c):
    x, y, z = (x + 4) % 4, (y + 4) % 4, (z + 4) % 4
    return (z * 4 + (y % 2) * 2 + c, (y // 2) * 4 + x)


def lanes(parts):
    return jnp.concatenate(parts, axis=1)


def rows(parts):
    return jnp.concatenate(parts, axis=0)


PARTS = ((0, 32), (32, 96))


def kernel(
    t_hbm, scr_ref, d_hbm, j_hbm, o_ref,
    tiles, metric, plain, owned, wants, wants_s, y_out0, y_out1, y_in0, y_in1, z_out0, z_out1, z_in0, z_in1, factor_t, perm,
    half, mid_x, mid_y, own, foll, fitted, diagonal, coupling, red_in, gathered,
    t_sem, j_sem, d_sem, sib_sem, w_sem, ws_sem, y_sem, z_sem, s1_out, s1_in, s2_out, s2_in, f_sem, r_sem, g_sem,
):
    x, y, z, c = place()
    y_out, y_in, z_out, z_in = (y_out0, y_out1), (y_in0, y_in1), (z_out0, z_out1), (z_in0, z_in1)

    load_d = pltpu.make_async_copy(d_hbm, plain, d_sem)
    load_d.start()
    load_t = []
    for g in range(2):
        span = pl.ds(g * 64, 64)
        load_t.append(pltpu.make_async_copy(t_hbm.at[:, span], tiles.at[:, span], t_sem.at[g]))
    load_j = pltpu.make_async_copy(j_hbm, metric, j_sem)
    for copy in load_t:
        copy.start()
    load_j.start()

    wants[0, z, pl.ds(0, 4), pl.ds(0, 3)] = scr_ref[...]

    plane = [(dx, dy) for dx in range(4) for dy in range(4) if (dx, dy) != (0, 0)]
    above = [(dy, dz) for dy in (1, 3, 0) for dz in (0, 1, 2, 3) if (dy, dz) != (0, 0)]
    barrier = pltpu.get_barrier_semaphore()
    peers = [device(x, y, z, 1 - c), device(x, y, z + 2 * c - 1, 1 - c)]
    peers += [device(x, y + dy, z + dz, c) for dy, dz in above if dz]
    peers += [device(x + dx, y + dy, z, c) for dx, dy in plane]
    for peer in peers:
        pl.semaphore_signal(barrier, inc=1, device_id=peer, device_id_type=MESH)

    r = lax.broadcasted_iota(jnp.int32, (256, 256), 0)
    k = lax.broadcasted_iota(jnp.int32, (256, 256), 1)
    perm[...] = jnp.where((r % 16) * 16 + r // 16 == k, 1.0, 0.0).astype(BF16)
    diagonal[...] = jnp.zeros_like(diagonal)
    coupling[...] = jnp.zeros_like(coupling)

    load_d.wait()

    @pl.loop(0, 8)
    def _(n):
        for e in range(4):
            owned[c * 32 + n * 4 + e] = plain[n * 4 + e].T

    pl.semaphore_wait(barrier, len(peers))

    def remote(src, dst, send, recv, peer):
        copy = pltpu.make_async_remote_copy(
            src_ref=src, dst_ref=dst, send_sem=send, recv_sem=recv, device_id=peer, device_id_type=MESH
        )
        copy.start()
        return copy

    def done(sem, ref):
        pltpu.make_async_copy(ref, ref, sem).wait()

    for n, (dy, dz) in enumerate(above):
        slot = {0: 0, 1: 1, 3: 2}[dy]
        group = 0 if dy else 1
        remote(wants.at[0, z], wants.at[slot, z], w_sem.at[0, group], w_sem.at[1, group], device(x, y + dy, z + dz, c))
    span = pl.ds(c * 32, 32)
    sibling = remote(owned.at[span], owned.at[span], sib_sem.at[0], sib_sem.at[1], device(x, y, z, 1 - c))
    others, column = pl.ds(1, 2), pl.ds(0, 3)
    done(w_sem.at[1, 0], wants.at[others])
    others_s = pltpu.make_async_copy(wants.at[others], wants_s.at[others], ws_sem.at[0])
    others_s.start()
    done(w_sem.at[1, 1], wants.at[0, column])
    column_s = pltpu.make_async_copy(wants.at[0], wants_s.at[0], ws_sem.at[1])
    column_s.start()
    sibling.wait_recv()
    others_s.wait()

    first = (z * 4 + (y % 2) * 2) * 32

    def pick(column, zz, slot, part):
        block = wants_s[column, zz, slot, 1] - first
        inside = (block >= 0) & (block < 64)
        start, count = PARTS[part]
        found = owned[jnp.clip(block, 0, 63), pl.ds(start, count), :]
        return jnp.where(inside, found, jnp.zeros_like(found))

    for part in range(2):
        for way in range(2):
            @pl.loop(0, 4)
            def _(zz):
                for sub in range(2):
                    y_out[part][way, zz, sub] = pick(2 - way, zz, way * 2 + sub, part)

            remote(
                y_out[part].at[way], y_in[part].at[way], y_sem.at[0, part], y_sem.at[1, part],
                device(x, y + 1 - 2 * way, z, c),
            )
    column_s.wait()

    def along_z(part):
        done(y_sem.at[1, part], y_in[part])
        for way in range(2):
            @pl.loop(0, 4)
            def _(zz):
                for sub in range(2):
                    z_out[part][zz, way * 2 + sub] = pick(0, zz, way * 2 + sub, part) + y_in[part][way, zz, sub]

        for dz in (2, 1, 3):
            remote(
                z_out[part].at[(z + dz) % 4], z_in[part].at[dz - 1], z_sem.at[0, part], z_sem.at[1, part],
                device(x, y, z + dz, c),
            )

    def arrived(part):
        done(z_sem.at[1, part], z_in[part])
        start, count = PARTS[part]
        for slot in range(4):
            block = z_out[part][z, slot]
            for dz in range(3):
                block = block + z_in[part][dz, slot]
            factor_t[pl.ds(start, count), pl.ds(slot * B, B)] = block

    def transform(part, low, high):
        start, count = PARTS[part]

        @pl.loop(low, high)
        def _(g):
            made = []
            for pair in range(8):
                m = g * 16 + pair * 2
                right = rows([lanes([tiles[t, m], tiles[t, m + 1]]) for t in range(4)])
                out = jnp.dot(
                    factor_t[pl.ds(start, count), :], right, preferred_element_type=F32
                ).astype(BF16)
                made += [out[:, :B], out[:, B:]]
            for group in range(0, count // 16, 2):
                stack = lanes([rows([one[(group + e) * 16:(group + e + 1) * 16] for one in made]) for e in range(2)])
                turned = jnp.dot(perm[...], stack, preferred_element_type=F32).astype(BF16)
                for e in range(2):
                    for i in range(16):
                        half[start + (group + e) * 16 + i, pl.ds(pl.multiple_of(g * 16, 16), 16), :] = turned[
                            i * 16:(i + 1) * 16, e * B:(e + 1) * B
                        ]

    def cut(h):
        return pl.ds(0, B) if h is None else pl.ds(h * 64, 64)

    def first_hop(chunk, h=None):
        n, odd, ms = chunk // 2, chunk % 2, cut(h)
        at = y if odd else x
        land = mid_y.at[n, y // 2, y % 2, :, ms] if odd else mid_x.at[n, x, :, ms]
        for d in (2, 1, 3):
            there = (at + d) % 4
            peer = device(x, y + d, z, c) if odd else device(x + d, y, z, c)
            remote(half.at[pl.ds(chunk * 16 + there * 4, 4), ms], land, s1_out.at[n], s1_in.at[chunk], peer)
        pltpu.make_async_copy(half.at[pl.ds(chunk * 16 + at * 4, 4), ms], land, s1_in.at[chunk]).start()

    def second_hop(chunk, h=None):
        n, odd, ms = chunk // 2, chunk % 2, cut(h)
        into = chunk if h is None else 6 + 2 * h + odd
        at = x if odd else y
        land = own.at[chunk, :, :, x, ms] if odd else own.at[chunk, y // 2, y % 2, :, ms]
        for d in (2, 1, 3):
            there = (at + d) % 4
            peer = device(x + d, y, z, c) if odd else device(x, y + d, z, c)
            source = mid_y.at[n, :, :, there, ms] if odd else mid_x.at[n, :, there, ms]
            remote(source, land, s2_out.at[n], s2_in.at[into], peer)
        source = mid_y.at[n, :, :, at, ms] if odd else mid_x.at[n, :, at, ms]
        pltpu.make_async_copy(source, land, s2_in.at[into]).start()

    def follow(chunk, h=None):
        ms, sem = cut(h), chunk // 2 + (h or 0)
        remote(
            own.at[chunk, :, c, :, ms], foll.at[chunk, 1, :, :, ms], f_sem.at[0, sem], f_sem.at[1, sem],
            device(x, y, z - (1 - c), 1 - c),
        )
        remote(
            own.at[chunk, :, 1 - c, :, ms], foll.at[chunk, 0, :, :, ms], f_sem.at[0, sem], f_sem.at[1, sem],
            device(x, y, z, 1 - c),
        )

    def first_done(pair):
        done(s1_in.at[pair * 2], mid_x.at[pair])
        done(s1_in.at[pair * 2 + 1], mid_y.at[pair])

    def second_done(pair, h=None):
        size = own.at[0, :, :, :, cut(h)]
        for e in range(2):
            done(s2_in.at[pair * 2 + e + 2 * (h or 0)], size)

    def follow_done(pair, h=None):
        done(f_sem.at[1, pair + (h or 0)], foll.at[pl.ds(0, 2), :, :, :, cut(h)])

    def both(hop, pair, h=None):
        for e in range(2):
            hop(pair * 2 + e, h)

    def own_rows(chunk, s):
        return lanes([own[chunk, g, s, e] for g in range(2) for e in range(4)])

    def foll_rows(chunk, s):
        return lanes([foll[chunk, s, g, e] for g in range(2) for e in range(4)])

    def across(left, right):
        return lax.dot_general(left, right, (((1,), (1,)), ((), ())), preferred_element_type=F32)

    def with_itself(pair):
        for e in range(2):
            chunk = pair * 2 + e
            stack = rows([own_rows(chunk, s) for s in range(2)])
            fitted[pair % 2, e] = jnp.dot(stack, metric[...], preferred_element_type=F32).astype(BF16)
            for s in range(2):
                diagonal[s] += across(fitted[pair % 2, e, pl.ds(s * B, B), :], own_rows(chunk, s))

    def with_next(pair):
        for e in range(2):
            for s in range(2):
                coupling[s] += across(fitted[pair % 2, e, pl.ds(s * B, B), :], foll_rows(pair * 2 + e, s))

    along_z(0)
    along_z(1)
    arrived(0)
    load_t[0].wait()
    transform(0, 0, 4)
    both(first_hop, 0, 0)
    load_t[1].wait()
    transform(0, 4, 8)
    both(first_hop, 0, 1)
    arrived(1)
    transform(1, 0, 4)
    both(first_hop, 1, 0)
    transform(1, 4, 6)
    first_done(0)
    both(second_hop, 0)
    transform(1, 6, 8)
    both(first_hop, 1, 1)
    both(first_hop, 2)
    load_j.wait()
    first_done(1)
    both(second_hop, 1)
    both(first_hop, 3)
    second_done(0)
    both(follow, 0)
    with_itself(0)
    first_done(2)
    both(second_hop, 2)
    follow_done(0)
    with_next(0)
    second_done(1)
    both(follow, 1)
    with_itself(1)
    first_done(3)
    both(second_hop, 3, 0)
    both(second_hop, 3, 1)
    follow_done(1)
    with_next(1)
    second_done(2)
    both(follow, 2)
    with_itself(2)
    second_done(3, 0)
    both(follow, 3, 0)
    follow_done(2)
    with_next(2)
    second_done(3, 1)
    both(follow, 3, 1)
    with_itself(3)

    def share(xx, yy):
        return pl.ds(pl.multiple_of((((yy + 4) % 4) // 2 * 4 + (xx + 4) % 4) * 16, 16), 16)

    def scatter(which, summand):
        for n, (dx, dy) in enumerate(plane):
            remote(
                summand.at[(y + dy) % 2, share(x + dx, y + dy)], red_in.at[which, n],
                r_sem.at[0, which], r_sem.at[1, which], device(x + dx, y + dy, z, c),
            )

    def collect(which, summand):
        result = summand[y % 2, share(x, y), :]
        done(r_sem.at[1, which], red_in.at[which])
        for n in range(len(plane)):
            result = result + red_in[which, n]
        gathered[share(x, y), pl.ds(which * B, B)] = result.astype(BF16)

    scatter(0, diagonal)
    follow_done(3, 0)
    follow_done(3, 1)
    with_next(3)
    scatter(1, coupling)
    collect(0, diagonal)
    collect(1, coupling)
    for dx, dy in plane:
        if dy % 2 == 0:
            remote(
                gathered.at[share(x, y)], gathered.at[share(x, y)], g_sem.at[0], g_sem.at[1],
                device(x + dx, y + dy, z, c),
            )

    done(w_sem.at[0, 0], wants.at[others])
    done(w_sem.at[0, 1], wants.at[0, column])
    sibling.wait_send()
    for part in range(2):
        done(y_sem.at[0, part], y_in[part])
        done(z_sem.at[0, part], z_in[part])
    for pair in range(4):
        done(s1_out.at[pair], half.at[pl.ds(0, 24)])
        done(s2_out.at[pair], half.at[pl.ds(0, 24)])
    for pair in range(3):
        done(f_sem.at[0, pair], foll.at[pl.ds(0, 2)])
    for h in range(2):
        done(f_sem.at[0, 3 + h], foll.at[pl.ds(0, 2), :, :, :, cut(h)])
    for which in range(2):
        done(r_sem.at[0, which], red_in.at[which])
    rest = gathered.at[pl.ds(0, 112)]
    done(g_sem.at[0], rest)
    done(g_sem.at[1], rest)
    o_ref[...] = gathered[...]


def on_device(three_center, screening, density_factor, metric_inverse):
    dma = pltpu.SemaphoreType.DMA
    return pl.pallas_call(
        kernel,
        out_shape=jax.ShapeDtypeStruct((B, 2 * B), BF16),
        in_specs=[
            pl.BlockSpec(memory_space=pl.ANY),
            pl.BlockSpec(memory_space=pltpu.VMEM),
            pl.BlockSpec(memory_space=pl.ANY),
            pl.BlockSpec(memory_space=pl.ANY),
        ],
        out_specs=pl.BlockSpec(memory_space=pltpu.VMEM),
        scratch_shapes=[
            pltpu.VMEM((4, B, B, B), BF16),
            pltpu.VMEM((1024, 1024), BF16),
            pltpu.VMEM((32, B, B), BF16),
            pltpu.VMEM((64, B, B), BF16),
            pltpu.VMEM((3, 4, 8, B), jnp.int32),
            pltpu.SMEM((3, 4, 8, B), jnp.int32),
            *[pltpu.VMEM((2, 4, 2, count, B), BF16) for _, count in PARTS],
            *[pltpu.VMEM((2, 4, 2, count, B), BF16) for _, count in PARTS],
            *[pltpu.VMEM((4, 4, count, B), BF16) for _, count in PARTS],
            *[pltpu.VMEM((3, 4, count, B), BF16) for _, count in PARTS],
            pltpu.VMEM((B, 4 * B), BF16),
            pltpu.VMEM((256, 256), BF16),
            pltpu.VMEM((B, B, B), BF16),
            pltpu.VMEM((4, 4, 4, B, B), BF16),
            pltpu.VMEM((4, 2, 2, 4, B, B), BF16),
            pltpu.VMEM((8, 2, 2, 4, B, B), BF16),
            pltpu.VMEM((8, 2, 2, 4, B, B), BF16),
            pltpu.VMEM((2, 2, 2 * B, 1024), BF16),
            pltpu.VMEM((2, B, B), F32),
            pltpu.VMEM((2, B, B), F32),
            pltpu.VMEM((2, 15, 16, B), F32),
            pltpu.VMEM((B, 2 * B), BF16),
            dma((2,)),
            dma,
            dma,
            dma((2,)),
            dma((2, 2)),
            dma((2,)),
            dma((2, 2)),
            dma((2, 2)),
            dma((4,)),
            dma((8,)),
            dma((4,)),
            dma((10,)),
            dma((2, 5)),
            dma((2, 2)),
            dma((2,)),
        ],
        compiler_params=pltpu.CompilerParams(
            collective_id=0, has_side_effects=True, vmem_limit_bytes=44 * 1024 * 1024
        ),
        cost_estimate=pl.CostEstimate(flops=8_000_000_000, bytes_accessed=20_000_000, transcendentals=0),
    )(three_center, screening, density_factor.reshape(-1, B, B), metric_inverse)


def solution(mesh):
    placed = (P(("orb", "aux"), None, None, None), P(("orb", "aux"), None), P("orb", None), P())
    return jax.shard_map(
        on_device, mesh=mesh, in_specs=placed, out_specs=P("orb", None), check_vma=False
    )
```

time: 102 us -> 96.3 us (0.944)
  Pallas kernels: 101 us -> 92 us
  local copies, waits for them, and re-layouts: 1.47 us -> 4.13 us
    pallas_call x1, Pallas kernels: 101 us -> 92 us  [on_device(): pl.pallas_call(kernel, out_shape=jax.ShapeDtypeStruct((B, 2 * B), BF16),...]
    unnamed x1 -> x7, local copies, waits for them, and re-layouts: 1.47 us -> 4.13 us
where the time goes in v2:
time: 96.3 us; the launch traced here: 96.2 us
  Pallas kernels  92 us (96%)
  local copies, waits for them, and re-layouts  4.13 us (4%)
    pallas_call x1, Pallas kernels, on_device(): pl.pallas_call(kernel, out_shape=jax.ShapeDtypeStruct((B, 2 * B), BF16),...  92 us
    unnamed x7, local copies, waits for them, and re-layouts  4.13 us

profile of v2, /device:TPU:1, one launch (start us, length us, event | category | flops | bytes accessed | tf_op | source)
XLA Modules:
  0.0 96.2 jit_solution(10819616268617082913)
XLA Ops:
  0.0 0.0 copy-start
  0.0 1.6 %copy-done = bf16[1024,1024]{1,0:T(8,128)(2,1)S(1)} copy-done((bf16[1024,1024]{1,0:T(8,128)(2,1)S(1)}, bf16[1024,1024]{1,0:T(8,128)(2,1)}, u32[]{:S(2)}) %copy-start) | copy-done | bytes 2097176
  1.6 0.0 copy-start.1
  1.6 1.2 %copy-done.1 = bf16[4096,128]{1,0:T(8,128)(2,1)S(1)} copy-done((bf16[4096,128]{1,0:T(8,128)(2,1)S(1)}, bf16[4096,128]{1,0:T(8,128)(2,1)}, u32[]{:S(2)}) %copy-start.1) | copy-done | bytes 1048600
  2.8 0.0 copy-start.2
  2.8 0.7 copy-done.2
  3.5 92.0 %shard_map.46 = bf16[128,256]{1,0:T(8,128)(2,1)S(1)} custom-call(bf16[4,128,128,128]{3,2,1,0:T(8,128)(2,1)} %t_hbm.1, s32[4,3]{1,0:T(4,128)S(1)} %copy-done.2, bf16[32,128,128]{2,1,0:T(8,128)(2,1)S(1)} %bitcast.1, bf16[1024,1024]{1,0:T(8,128)(2,1)S(1)} %copy-done), custom_call_target="tpu_custom_call" | custom-call | flops 8000000000 | bytes 20000000 | tf_op jit(solution)/shard_map/pallas_call | solution.py:351
  95.5 0.6 copy.6
Async XLA Ops:
  0.0 1.6 %copy-start = (bf16[1024,1024]{1,0:T(8,128)(2,1)S(1)}, bf16[1024,1024]{1,0:T(8,128)(2,1)}, u32[]{:S(2)}) copy-start(bf16[1024,1024]{1,0:T(8,128)(2,1)} %j_hbm.1) | copy-start | bytes 6291460
  1.6 1.2 %copy-start.1 = (bf16[4096,128]{1,0:T(8,128)(2,1)S(1)}, bf16[4096,128]{1,0:T(8,128)(2,1)}, u32[]{:S(2)}) copy-start(bf16[4096,128]{1,0:T(8,128)(2,1)} %param.6) | copy-start | bytes 3145732
  2.8 0.7 copy-start.2

commit v3 on v2

--- a/solution.py
+++ b/solution.py
@@ -48,9 +48,6 @@
         span = pl.ds(g * 64, 64)
         load_t.append(pltpu.make_async_copy(t_hbm.at[:, span], tiles.at[:, span], t_sem.at[g]))
     load_j = pltpu.make_async_copy(j_hbm, metric, j_sem)
-    for copy in load_t:
-        copy.start()
-    load_j.start()
 
     wants[0, z, pl.ds(0, 4), pl.ds(0, 3)] = scr_ref[...]
 
@@ -70,6 +67,7 @@
     coupling[...] = jnp.zeros_like(coupling)
 
     load_d.wait()
+    load_t[0].start()
 
     @pl.loop(0, 8)
     def _(n):
@@ -115,7 +113,7 @@
 
     for part in range(2):
         for way in range(2):
-            @pl.loop(0, 4)
+            @pl.loop(0, 4, unroll=True)
             def _(zz):
                 for sub in range(2):
                     y_out[part][way, zz, sub] = pick(2 - way, zz, way * 2 + sub, part)
@@ -125,11 +123,13 @@
                 device(x, y + 1 - 2 * way, z, c),
             )
     column_s.wait()
+    load_t[1].start()
+    load_j.start()
 
     def along_z(part):
         done(y_sem.at[1, part], y_in[part])
         for way in range(2):
-            @pl.loop(0, 4)
+            @pl.loop(0, 4, unroll=True)
             def _(zz):
                 for sub in range(2):
                     z_out[part][zz, way * 2 + sub] = pick(0, zz, way * 2 + sub, part) + y_in[part][way, zz, sub]
@@ -174,28 +174,28 @@
     def cut(h):
         return pl.ds(0, B) if h is None else pl.ds(h * 64, 64)
 
-    def first_hop(chunk, h=None):
+    def first_hop(chunk, d, h=None):
         n, odd, ms = chunk // 2, chunk % 2, cut(h)
         at = y if odd else x
         land = mid_y.at[n, y // 2, y % 2, :, ms] if odd else mid_x.at[n, x, :, ms]
-        for d in (2, 1, 3):
-            there = (at + d) % 4
+        source = half.at[pl.ds(chunk * 16 + (at + d) % 4 * 4, 4), ms]
+        if d:
             peer = device(x, y + d, z, c) if odd else device(x + d, y, z, c)
-            remote(half.at[pl.ds(chunk * 16 + there * 4, 4), ms], land, s1_out.at[n], s1_in.at[chunk], peer)
-        pltpu.make_async_copy(half.at[pl.ds(chunk * 16 + at * 4, 4), ms], land, s1_in.at[chunk]).start()
-
-    def second_hop(chunk, h=None):
+            remote(source, land, s1_out.at[n], s1_in.at[chunk], peer)
+        else:
+            pltpu.make_async_copy(source, land, s1_in.at[chunk]).start()
+
+    def second_hop(chunk, d, h=None):
         n, odd, ms = chunk // 2, chunk % 2, cut(h)
         into = chunk if h is None else 6 + 2 * h + odd
-        at = x if odd else y
+        there = ((x if odd else y) + d) % 4
         land = own.at[chunk, :, :, x, ms] if odd else own.at[chunk, y // 2, y % 2, :, ms]
-        for d in (2, 1, 3):
-            there = (at + d) % 4
+        source = mid_y.at[n, :, :, there, ms] if odd else mid_x.at[n, :, there, ms]
+        if d:
             peer = device(x + d, y, z, c) if odd else device(x, y + d, z, c)
-            source = mid_y.at[n, :, :, there, ms] if odd else mid_x.at[n, :, there, ms]
             remote(source, land, s2_out.at[n], s2_in.at[into], peer)
-        source = mid_y.at[n, :, :, at, ms] if odd else mid_x.at[n, :, at, ms]
-        pltpu.make_async_copy(source, land, s2_in.at[into]).start()
+        else:
+            pltpu.make_async_copy(source, land, s2_in.at[into]).start()
 
     def follow(chunk, h=None):
         ms, sem = cut(h), chunk // 2 + (h or 0)
@@ -221,8 +221,13 @@
         done(f_sem.at[1, pair + (h or 0)], foll.at[pl.ds(0, 2), :, :, :, cut(h)])
 
     def both(hop, pair, h=None):
+        for d in (1, 3, 2, 0):
+            for e in range(2):
+                hop(pair * 2 + e, d, h)
+
+    def follow_both(pair, h=None):
         for e in range(2):
-            hop(pair * 2 + e, h)
+            follow(pair * 2 + e, h)
 
     def own_rows(chunk, s):
         return lanes([own[chunk, g, s, e] for g in range(2) for e in range(4)])
@@ -247,10 +252,11 @@
                 coupling[s] += across(fitted[pair % 2, e, pl.ds(s * B, B), :], foll_rows(pair * 2 + e, s))
 
     along_z(0)
-    along_z(1)
     arrived(0)
     load_t[0].wait()
-    transform(0, 0, 4)
+    transform(0, 0, 2)
+    along_z(1)
+    transform(0, 2, 4)
     both(first_hop, 0, 0)
     load_t[1].wait()
     transform(0, 4, 8)
@@ -258,10 +264,9 @@
     arrived(1)
     transform(1, 0, 4)
     both(first_hop, 1, 0)
-    transform(1, 4, 6)
     first_done(0)
     both(second_hop, 0)
-    transform(1, 6, 8)
+    transform(1, 4, 8)
     both(first_hop, 1, 1)
     both(first_hop, 2)
     load_j.wait()
@@ -269,14 +274,14 @@
     both(second_hop, 1)
     both(first_hop, 3)
     second_done(0)
-    both(follow, 0)
+    follow_both(0)
     with_itself(0)
     first_done(2)
     both(second_hop, 2)
     follow_done(0)
     with_next(0)
     second_done(1)
-    both(follow, 1)
+    follow_both(1)
     with_itself(1)
     first_done(3)
     both(second_hop, 3, 0)
@@ -284,14 +289,14 @@
     follow_done(1)
     with_next(1)
     second_done(2)
-    both(follow, 2)
+    follow_both(2)
     with_itself(2)
     second_done(3, 0)
-    both(follow, 3, 0)
+    follow_both(3, 0)
     follow_done(2)
     with_next(2)
     second_done(3, 1)
-    both(follow, 3, 1)
+    follow_both(3, 1)
     with_itself(3)
 
     def share(xx, yy):
@@ -398,7 +403,7 @@
             dma((2,)),
         ],
         compiler_params=pltpu.CompilerParams(
-            collective_id=0, has_side_effects=True, vmem_limit_bytes=44 * 1024 * 1024
+            collective_id=0, has_side_effects=True, vmem_limit_bytes=54 * 1024 * 1024
         ),
         cost_estimate=pl.CostEstimate(flops=8_000_000_000, bytes_accessed=20_000_000, transcendentals=0),
     )(three_center, screening, density_factor.reshape(-1, B, B), metric_inverse)

time: 96.3 us -> 94.8 us (0.984)
  local copies, waits for them, and re-layouts: 4.13 us -> 1.47 us
  Pallas kernels: 92 us -> 93.1 us
    unnamed x7 -> x1, local copies, waits for them, and re-layouts: 4.13 us -> 1.47 us
    pallas_call x1, Pallas kernels: 92 us -> 93.1 us  [on_device(): pl.pallas_call(kernel, out_shape=jax.ShapeDtypeStruct((B, 2 * B), BF16),...]
where the time goes in v3:
time: 94.8 us; the launch traced here: 94.5 us
  Pallas kernels  93.1 us (98%)
  local copies, waits for them, and re-layouts  1.47 us (2%)
    pallas_call x1, Pallas kernels, on_device(): pl.pallas_call(kernel, out_shape=jax.ShapeDtypeStruct((B, 2 * B), BF16),...  93.1 us

profile of v3, /device:TPU:1, one launch (start us, length us, event | category | flops | bytes accessed | tf_op | source)
XLA Modules:
  0.0 94.5 jit_solution(14242694376673814685)
XLA Ops:
  0.0 93.1 %shard_map.46 = bf16[128,256]{1,0:T(8,128)(2,1)} custom-call(bf16[4,128,128,128]{3,2,1,0:T(8,128)(2,1)} %t_hbm.1, s32[4,3]{1,0:T(4,128)} %scr_ref.1, bf16[32,128,128]{2,1,0:T(8,128)(2,1)} %bitcast.1, bf16[1024,1024]{1,0:T(8,128)(2,1)} %j_hbm.1), custom_call_target="tpu_custom_call" | custom-call | flops 8000000000 | bytes 20000000 | tf_op jit(solution)/shard_map/pallas_call | solution.py:356
  93.1 1.5 %copy.6 = bf16[128,256]{1,0:T(8,128)(2,1)} copy(bf16[128,256]{1,0:T(8,128)(2,1)} %shard_map.46) | data formatting | bytes 131072

commit v4 on v3

--- a/solution.py
+++ b/solution.py
@@ -29,17 +29,19 @@
     return jnp.concatenate(parts, axis=0)
 
 
-PARTS = ((0, 32), (32, 96))
+PARTS = ((0, 32), (32, 32), (64, 64))
 
 
 def kernel(
     t_hbm, scr_ref, d_hbm, j_hbm, o_ref,
-    tiles, metric, plain, owned, wants, wants_s, y_out0, y_out1, y_in0, y_in1, z_out0, z_out1, z_in0, z_in1, factor_t, perm,
+    tiles, metric, plain, owned, wants, wants_s, y_out0, y_out1, y_out2, y_in0, y_in1, y_in2,
+    z_out0, z_out1, z_out2, z_in0, z_in1, z_in2, factor_t, perm,
     half, mid_x, mid_y, own, foll, fitted, diagonal, coupling, red_in, gathered,
     t_sem, j_sem, d_sem, sib_sem, w_sem, ws_sem, y_sem, z_sem, s1_out, s1_in, s2_out, s2_in, f_sem, r_sem, g_sem,
 ):
     x, y, z, c = place()
-    y_out, y_in, z_out, z_in = (y_out0, y_out1), (y_in0, y_in1), (z_out0, z_out1), (z_in0, z_in1)
+    y_out, y_in = (y_out0, y_out1, y_out2), (y_in0, y_in1, y_in2)
+    z_out, z_in = (z_out0, z_out1, z_out2), (z_in0, z_in1, z_in2)
 
     load_d = pltpu.make_async_copy(d_hbm, plain, d_sem)
     load_d.start()
@@ -111,7 +113,7 @@
         found = owned[jnp.clip(block, 0, 63), pl.ds(start, count), :]
         return jnp.where(inside, found, jnp.zeros_like(found))
 
-    for part in range(2):
+    for part in range(3):
         for way in range(2):
             @pl.loop(0, 4, unroll=True)
             def _(zz):
@@ -172,7 +174,10 @@
                         ]
 
     def cut(h):
-        return pl.ds(0, B) if h is None else pl.ds(h * 64, 64)
+        return {None: pl.ds(0, B), 0: pl.ds(0, 64), 1: pl.ds(64, 64), 2: pl.ds(0, 32), 3: pl.ds(32, 32), 4: pl.ds(64, 32), 5: pl.ds(96, 32)}[h]
+
+    def piece(h):
+        return {None: 0, 0: 0, 4: 1, 5: 2}[h]
 
     def first_hop(chunk, d, h=None):
         n, odd, ms = chunk // 2, chunk % 2, cut(h)
@@ -187,7 +192,7 @@
 
     def second_hop(chunk, d, h=None):
         n, odd, ms = chunk // 2, chunk % 2, cut(h)
-        into = chunk if h is None else 6 + 2 * h + odd
+        into = chunk + 2 * piece(h)
         there = ((x if odd else y) + d) % 4
         land = own.at[chunk, :, :, x, ms] if odd else own.at[chunk, y // 2, y % 2, :, ms]
         source = mid_y.at[n, :, :, there, ms] if odd else mid_x.at[n, :, there, ms]
@@ -198,7 +203,7 @@
             pltpu.make_async_copy(source, land, s2_in.at[into]).start()
 
     def follow(chunk, h=None):
-        ms, sem = cut(h), chunk // 2 + (h or 0)
+        ms, sem = cut(h), chunk // 2 + piece(h)
         remote(
             own.at[chunk, :, c, :, ms], foll.at[chunk, 1, :, :, ms], f_sem.at[0, sem], f_sem.at[1, sem],
             device(x, y, z - (1 - c), 1 - c),
@@ -215,10 +220,10 @@
     def second_done(pair, h=None):
         size = own.at[0, :, :, :, cut(h)]
         for e in range(2):
-            done(s2_in.at[pair * 2 + e + 2 * (h or 0)], size)
+            done(s2_in.at[pair * 2 + e + 2 * piece(h)], size)
 
     def follow_done(pair, h=None):
-        done(f_sem.at[1, pair + (h or 0)], foll.at[pl.ds(0, 2), :, :, :, cut(h)])
+        done(f_sem.at[1, pair + piece(h)], foll.at[pl.ds(0, 2), :, :, :, cut(h)])
 
     def both(hop, pair, h=None):
         for d in (1, 3, 2, 0):
@@ -252,40 +257,47 @@
                 coupling[s] += across(fitted[pair % 2, e, pl.ds(s * B, B), :], foll_rows(pair * 2 + e, s))
 
     along_z(0)
+    along_z(1)
     arrived(0)
     load_t[0].wait()
     transform(0, 0, 2)
-    along_z(1)
+    both(first_hop, 0, 2)
+    along_z(2)
     transform(0, 2, 4)
-    both(first_hop, 0, 0)
+    both(first_hop, 0, 3)
     load_t[1].wait()
     transform(0, 4, 8)
     both(first_hop, 0, 1)
     arrived(1)
     transform(1, 0, 4)
     both(first_hop, 1, 0)
+    transform(1, 4, 6)
     first_done(0)
     both(second_hop, 0)
-    transform(1, 4, 8)
+    transform(1, 6, 8)
     both(first_hop, 1, 1)
-    both(first_hop, 2)
-    load_j.wait()
+    arrived(2)
+    transform(2, 0, 4)
+    both(first_hop, 2, 0)
     first_done(1)
     both(second_hop, 1)
+    transform(2, 4, 8)
+    both(first_hop, 2, 1)
     both(first_hop, 3)
+    load_j.wait()
     second_done(0)
     follow_both(0)
-    with_itself(0)
     first_done(2)
     both(second_hop, 2)
+    with_itself(0)
+    second_done(1)
+    follow_both(1)
+    first_done(3)
+    for h in (0, 4, 5):
+        both(second_hop, 3, h)
+    with_itself(1)
     follow_done(0)
     with_next(0)
-    second_done(1)
-    follow_both(1)
-    with_itself(1)
-    first_done(3)
-    both(second_hop, 3, 0)
-    both(second_hop, 3, 1)
     follow_done(1)
     with_next(1)
     second_done(2)
@@ -295,8 +307,9 @@
     follow_both(3, 0)
     follow_done(2)
     with_next(2)
-    second_done(3, 1)
-    follow_both(3, 1)
+    for h in (4, 5):
+        second_done(3, h)
+        follow_both(3, h)
     with_itself(3)
 
     def share(xx, yy):
@@ -317,8 +330,8 @@
         gathered[share(x, y), pl.ds(which * B, B)] = result.astype(BF16)
 
     scatter(0, diagonal)
-    follow_done(3, 0)
-    follow_done(3, 1)
+    for h in (0, 4, 5):
+        follow_done(3, h)
     with_next(3)
     scatter(1, coupling)
     collect(0, diagonal)
@@ -333,7 +346,7 @@
     done(w_sem.at[0, 0], wants.at[others])
     done(w_sem.at[0, 1], wants.at[0, column])
     sibling.wait_send()
-    for part in range(2):
+    for part in range(3):
         done(y_sem.at[0, part], y_in[part])
         done(z_sem.at[0, part], z_in[part])
     for pair in range(4):
@@ -341,8 +354,8 @@
         done(s2_out.at[pair], half.at[pl.ds(0, 24)])
     for pair in range(3):
         done(f_sem.at[0, pair], foll.at[pl.ds(0, 2)])
-    for h in range(2):
-        done(f_sem.at[0, 3 + h], foll.at[pl.ds(0, 2), :, :, :, cut(h)])
+    for h in (0, 4, 5):
+        done(f_sem.at[0, 3 + piece(h)], foll.at[pl.ds(0, 2), :, :, :, cut(h)])
     for which in range(2):
         done(r_sem.at[0, which], red_in.at[which])
     rest = gathered.at[pl.ds(0, 112)]
@@ -392,18 +405,18 @@
             dma((2,)),
             dma((2, 2)),
             dma((2,)),
-            dma((2, 2)),
-            dma((2, 2)),
+            dma((2, 3)),
+            dma((2, 3)),
             dma((4,)),
             dma((8,)),
             dma((4,)),
-            dma((10,)),
-            dma((2, 5)),
+            dma((12,)),
+            dma((2, 6)),
             dma((2, 2)),
             dma((2,)),
         ],
         compiler_params=pltpu.CompilerParams(
-            collective_id=0, has_side_effects=True, vmem_limit_bytes=54 * 1024 * 1024
+            collective_id=0, has_side_effects=True, vmem_limit_bytes=int(53.5 * 1024 * 1024)
         ),
         cost_estimate=pl.CostEstimate(flops=8_000_000_000, bytes_accessed=20_000_000, transcendentals=0),
     )(three_center, screening, density_factor.reshape(-1, B, B), metric_inverse)

time: 94.8 us -> 93.1 us (0.982)
  Pallas kernels: 93.1 us -> 91.6 us
    pallas_call x1, Pallas kernels: 93.1 us -> 91.6 us  [on_device(): pl.pallas_call(kernel, out_shape=jax.ShapeDtypeStruct((B, 2 * B), BF16),...]
where the time goes in v4:
time: 93.1 us; the launch traced here: 92.9 us
  Pallas kernels  91.6 us (98%)
  local copies, waits for them, and re-layouts  1.31 us (1%)
    pallas_call x1, Pallas kernels, on_device(): pl.pallas_call(kernel, out_shape=jax.ShapeDtypeStruct((B, 2 * B), BF16),...  91.6 us

profile of v4, /device:TPU:1, one launch (start us, length us, event | category | flops | bytes accessed | tf_op | source)
XLA Modules:
  0.0 92.9 jit_solution(10419649330270902603)
XLA Ops:
  0.0 0.0 copy-start
  0.0 0.7 copy-done
  0.7 91.6 %shard_map.46 = bf16[128,256]{1,0:T(8,128)(2,1)S(1)} custom-call(bf16[4,128,128,128]{3,2,1,0:T(8,128)(2,1)} %t_hbm.1, s32[4,3]{1,0:T(4,128)S(1)} %copy-done, bf16[32,128,128]{2,1,0:T(8,128)(2,1)} %bitcast.1, bf16[1024,1024]{1,0:T(8,128)(2,1)} %j_hbm.1), custom_call_target="tpu_custom_call" | custom-call | flops 8000000000 | bytes 20000000 | tf_op jit(solution)/shard_map/pallas_call | solution.py:369
  92.3 0.6 copy.6
Async XLA Ops:
  0.0 0.7 copy-start

commit v5 on v4

--- a/solution.py
+++ b/solution.py
@@ -218,9 +218,9 @@
         done(s1_in.at[pair * 2 + 1], mid_y.at[pair])
 
     def second_done(pair, h=None):
-        size = own.at[0, :, :, :, cut(h)]
         for e in range(2):
-            done(s2_in.at[pair * 2 + e + 2 * piece(h)], size)
+            done(s2_in.at[pair * 2 + e + 2 * piece(h)], own.at[0, :, :, :, cut(h)])
+            follow(pair * 2 + e, h)
 
     def follow_done(pair, h=None):
         done(f_sem.at[1, pair + piece(h)], foll.at[pl.ds(0, 2), :, :, :, cut(h)])
@@ -229,10 +229,6 @@
         for d in (1, 3, 2, 0):
             for e in range(2):
                 hop(pair * 2 + e, d, h)
-
-    def follow_both(pair, h=None):
-        for e in range(2):
-            follow(pair * 2 + e, h)
 
     def own_rows(chunk, s):
         return lanes([own[chunk, g, s, e] for g in range(2) for e in range(4)])
@@ -286,12 +282,10 @@
     both(first_hop, 3)
     load_j.wait()
     second_done(0)
-    follow_both(0)
     first_done(2)
     both(second_hop, 2)
     with_itself(0)
     second_done(1)
-    follow_both(1)
     first_done(3)
     for h in (0, 4, 5):
         both(second_hop, 3, h)
@@ -301,15 +295,12 @@
     follow_done(1)
     with_next(1)
     second_done(2)
-    follow_both(2)
     with_itself(2)
     second_done(3, 0)
-    follow_both(3, 0)
     follow_done(2)
     with_next(2)
     for h in (4, 5):
         second_done(3, h)
-        follow_both(3, h)
     with_itself(3)
 
     def share(xx, yy):

time: 93.1 us -> 92.9 us (level)
  no operation moved by 1% of the time
where the time goes in v5:
time: 92.9 us; the launch traced here: 92.7 us
  Pallas kernels  91.4 us (98%)
  local copies, waits for them, and re-layouts  1.31 us (1%)
    pallas_call x1, Pallas kernels, on_device(): pl.pallas_call(kernel, out_shape=jax.ShapeDtypeStruct((B, 2 * B), BF16),...  91.4 us

profile of v5, /device:TPU:1, one launch (start us, length us, event | category | flops | bytes accessed | tf_op | source)
XLA Modules:
  0.0 92.7 jit_solution(14304992644350958986)
XLA Ops:
  0.0 0.0 copy-start
  0.0 0.7 copy-done
  0.7 91.4 %shard_map.46 = bf16[128,256]{1,0:T(8,128)(2,1)S(1)} custom-call(bf16[4,128,128,128]{3,2,1,0:T(8,128)(2,1)} %t_hbm.1, s32[4,3]{1,0:T(4,128)S(1)} %copy-done, bf16[32,128,128]{2,1,0:T(8,128)(2,1)} %bitcast.1, bf16[1024,1024]{1,0:T(8,128)(2,1)} %j_hbm.1), custom_call_target="tpu_custom_call" | custom-call | flops 8000000000 | bytes 20000000 | tf_op jit(solution)/shard_map/pallas_call | solution.py:360
  92.1 0.6 copy.6
Async XLA Ops:
  0.0 0.7 copy-start

commit v6 on v5

--- a/solution.py
+++ b/solution.py
@@ -177,7 +177,7 @@
         return {None: pl.ds(0, B), 0: pl.ds(0, 64), 1: pl.ds(64, 64), 2: pl.ds(0, 32), 3: pl.ds(32, 32), 4: pl.ds(64, 32), 5: pl.ds(96, 32)}[h]
 
     def piece(h):
-        return {None: 0, 0: 0, 4: 1, 5: 2}[h]
+        return {None: 0, 0: 0, 4: 1, 5: 2, 1: 4}[h]
 
     def first_hop(chunk, d, h=None):
         n, odd, ms = chunk // 2, chunk % 2, cut(h)
@@ -283,7 +283,8 @@
     load_j.wait()
     second_done(0)
     first_done(2)
-    both(second_hop, 2)
+    both(second_hop, 2, 0)
+    both(second_hop, 2, 1)
     with_itself(0)
     second_done(1)
     first_done(3)
@@ -294,10 +295,12 @@
     with_next(0)
     follow_done(1)
     with_next(1)
-    second_done(2)
+    second_done(2, 0)
+    second_done(2, 1)
     with_itself(2)
     second_done(3, 0)
-    follow_done(2)
+    follow_done(2, 0)
+    follow_done(2, 1)
     with_next(2)
     for h in (4, 5):
         second_done(3, h)
@@ -343,8 +346,10 @@
     for pair in range(4):
         done(s1_out.at[pair], half.at[pl.ds(0, 24)])
         done(s2_out.at[pair], half.at[pl.ds(0, 24)])
-    for pair in range(3):
+    for pair in range(2):
         done(f_sem.at[0, pair], foll.at[pl.ds(0, 2)])
+    for h in range(2):
+        done(f_sem.at[0, 2 + piece(h)], foll.at[pl.ds(0, 2), :, :, :, cut(h)])
     for h in (0, 4, 5):
         done(f_sem.at[0, 3 + piece(h)], foll.at[pl.ds(0, 2), :, :, :, cut(h)])
     for which in range(2):
@@ -401,8 +406,8 @@
             dma((4,)),
             dma((8,)),
             dma((4,)),
-            dma((12,)),
-            dma((2, 6)),
+            dma((14,)),
+            dma((2, 7)),
             dma((2, 2)),
             dma((2,)),
         ],

time: 92.9 us -> 90.9 us (0.978)
  Pallas kernels: 91.4 us -> 89.4 us
    pallas_call x1, Pallas kernels: 91.4 us -> 89.4 us  [on_device(): pl.pallas_call(kernel, out_shape=jax.ShapeDtypeStruct((B, 2 * B), BF16),...]
where the time goes in v6:
time: 90.9 us; the launch traced here: 90.8 us
  Pallas kernels  89.4 us (98%)
  local copies, waits for them, and re-layouts  1.31 us (1%)
    pallas_call x1, Pallas kernels, on_device(): pl.pallas_call(kernel, out_shape=jax.ShapeDtypeStruct((B, 2 * B), BF16),...  89.4 us

profile of v6, /device:TPU:1, one launch (start us, length us, event | category | flops | bytes accessed | tf_op | source)
XLA Modules:
  0.0 90.8 jit_solution(17648711581362053560)
XLA Ops:
  0.0 0.0 copy-start
  0.0 0.7 copy-done
  0.7 89.4 %shard_map.46 = bf16[128,256]{1,0:T(8,128)(2,1)S(1)} custom-call(bf16[4,128,128,128]{3,2,1,0:T(8,128)(2,1)} %t_hbm.1, s32[4,3]{1,0:T(4,128)S(1)} %copy-done, bf16[32,128,128]{2,1,0:T(8,128)(2,1)} %bitcast.1, bf16[1024,1024]{1,0:T(8,128)(2,1)} %j_hbm.1), custom_call_target="tpu_custom_call" | custom-call | flops 8000000000 | bytes 20000000 | tf_op jit(solution)/shard_map/pallas_call | solution.py:365
  90.1 0.6 copy.6
Async XLA Ops:
  0.0 0.7 copy-start
